TPU v7x, 32 devices: a whole 2x2x4 slice. The times are simulated.
32 devices in a mesh: rows: 16 (over z, y, x), batch: 2 (over core).
Axes of the slice: x: 2, y: 2, z: 4, core: 2. Of those that a mesh axis runs over, the one named last changes fastest.
Arguments:
- frames: bfloat16 [4096, 1024], P('rows', 'batch'), may hold values from -40 to 40
- tap_table: int32 [63], replicated, may hold values from -128 to 127
- sketch_matrix: bfloat16 [512, 256], replicated, may hold values from -0.25 to 0.25
- decay_rates: float32 [2, 256], P('batch'), may hold values from 0.5 to 1
Outputs:
- basis: float32 [2, 4096, 256], P('batch', 'rows')
- factor: float32 [2, 256, 256], P('batch')
- coeffs: float32 [2, 256, 512], P('batch')
All inputs are finite; a program needn't handle non-finite values.
Results may differ from a plain program's by a relative error of at most 0.0039.
The roundings to bfloat16 on the way count: a program that leaves them out, or rounds other values in their place, can miss the bound.
Values may be sent and summed in bfloat16 or wider, within the bound.
A program may use at most 64 MiB of HBM per device.

v0:
```python
import functools
import math

import jax
import jax.numpy as jnp
from jax import lax
from jax.experimental import pallas as pl
from jax.experimental.pallas import tpu as pltpu
from jax.sharding import PartitionSpec as P

MESH = pl.DeviceIdType.MESH
HIGHEST = lax.Precision.HIGHEST
F32 = jnp.float32
BF16 = jnp.bfloat16
LANES = 128
PANEL = 32
TILE = 8
GRANT = 63 * 1024 * 1024
HBM_SPEC = pl.BlockSpec(memory_space=pltpu.HBM)
VMEM_SPEC = pl.BlockSpec(memory_space=pltpu.VMEM)


def greet(count, batches, with_batch):
    row, turn = lax.axis_index("rows"), lax.axis_index("batch")
    barrier = pltpu.get_barrier_semaphore()
    for step in range(1, count):
        pl.semaphore_signal(
            barrier, inc=1, device_id=(lax.rem(row + step, count), turn), device_id_type=MESH
        )
    waits = count - 1
    if with_batch and batches > 1:

        @pl.when(turn > 0)
        def _():
            pl.semaphore_signal(barrier, inc=1, device_id=(row, turn - 1), device_id_type=MESH)

        @pl.when(turn < batches - 1)
        def _():
            pl.semaphore_signal(barrier, inc=1, device_id=(row, turn + 1), device_id_type=MESH)

        waits = waits + jnp.where(turn > 0, 1, 0) + jnp.where(turn < batches - 1, 1, 0)
    pl.semaphore_wait(barrier, waits)


def exchange(count, source_of, target_of, send_sems, recv_sems):
    row, turn = lax.axis_index("rows"), lax.axis_index("batch")
    copies = []
    for step in range(1, count):
        peer = lax.rem(row + step, count)
        copy = pltpu.make_async_remote_copy(
            src_ref=source_of(peer),
            dst_ref=target_of(row),
            send_sem=send_sems.at[step],
            recv_sem=recv_sems.at[step],
            device_id=(peer, turn),
            device_id_type=MESH,
        )
        copy.start()
        copies.append(copy)
    return copies


def groups(count):
    inner = 4 if count % 4 == 0 else 1
    return count // inner, inner


def send(source, target, send_sems, recv_sems, index, peer):
    copy = pltpu.make_async_remote_copy(
        src_ref=source,
        dst_ref=target,
        send_sem=send_sems.at[index],
        recv_sem=recv_sems.at[index],
        device_id=(peer, lax.axis_index("batch")),
        device_id_type=MESH,
    )
    copy.start()
    return copy


def place_of(count):
    inner = groups(count)[1]
    row = lax.axis_index("rows")
    return lax.div(row, inner), lax.rem(row, inner)


def gather(count, total, send_sems, recv_sems):
    outer, inner = groups(count)
    plane, spot = place_of(count)
    row = lax.axis_index("rows")
    across, within = [], []
    for o in range(1, outer):
        peer = lax.rem(plane + o, outer) * inner + spot
        across.append(send(total.at[row], total.at[row], send_sems, recv_sems, o * inner, peer))
    for o in range(outer):
        if o > 0:
            across[o - 1].wait_recv()
        owner = lax.rem(plane - o + outer, outer) * inner + spot
        for i in range(1, inner):
            peer = plane * inner + lax.rem(spot + i, inner)
            within.append(send(total.at[owner], total.at[owner], send_sems, recv_sems, o * inner + i, peer))
    return across, within


def cut(value, index, shard, dtype):
    low = index * shard
    if low < value.shape[0]:
        return value[low : low + shard]
    return jnp.zeros((shard, value.shape[1]), dtype)


def sum_slots(landed, copies):
    for copy in copies:
        copy.wait_recv()
    summed = landed[0]
    for sender in range(1, landed.shape[0]):
        summed = summed + landed[sender]
    return summed


def whole_kernel(
    count, batches, npoints,
    frames_hbm, taps_hbm, sketch_hbm, rates_hbm, basis_hbm, factor_hbm, coeffs,
    frames, taps, sketch, rates, tap_row, history, before, weighted, filtered,
    parts, landed, total, cross_parts, cross_landed, cross_mid, cross_last, cross_total, work, upper, inverse, basis, factor,
    load_sems, store_sems, hist_sems, prev_sems, gram_a, gram_b, gram_c, gram_d, cross_a, cross_b, cross_c, cross_d, cross_e, cross_f,
):
    row, turn = lax.axis_index("rows"), lax.axis_index("batch")
    frame_count = frames.shape[1]
    rank = sketch.shape[1]
    loads = [
        pltpu.make_async_copy(source, target, load_sems.at[index])
        for index, (source, target) in enumerate(
            ((taps_hbm, taps), (frames_hbm, frames), (sketch_hbm, sketch), (rates_hbm, rates))
        )
    ]
    for load in loads:
        load.start()
    greet(count, batches, True)

    def hist_copy():
        return pltpu.make_async_remote_copy(
            src_ref=frames_hbm.at[:, pl.ds(frame_count - LANES, LANES)],
            dst_ref=history,
            send_sem=hist_sems.at[0],
            recv_sem=hist_sems.at[1],
            device_id=(row, turn + 1),
            device_id_type=MESH,
        )

    def prev_copy():
        return pltpu.make_async_remote_copy(
            src_ref=weighted,
            dst_ref=before,
            send_sem=prev_sems.at[0],
            recv_sem=prev_sems.at[1],
            device_id=(row, turn + 1),
            device_id_type=MESH,
        )

    @pl.when(turn < batches - 1)
    def _():
        hist_copy().start()

    loads[0].wait()
    tap_row[...] = jnp.zeros_like(tap_row)
    tap_row[:, : taps.shape[1]] = taps[...].astype(F32) / 1024.0
    spread = jnp.broadcast_to(tap_row[...], (LANES, tap_row.shape[1]))
    rolled = pltpu.roll(spread, 0, 1, stride=1, stride_axis=0)
    wide = tap_row.shape[1]
    after = jnp.concatenate([rolled[:, wide - LANES :], rolled[:, :LANES]], axis=1)
    band = jnp.concatenate([rolled[:, LANES : 3 * LANES], rolled[:, : 2 * LANES], after], axis=0).astype(BF16)

    step = 2 * LANES
    loads[1].wait()
    for start in range(step, frame_count, step):
        filtered[:, start : start + step] = jnp.dot(
            frames[:, start - LANES : start + step], band, preferred_element_type=F32
        ).astype(BF16)
    here = jnp.dot(frames[:, :step], band[LANES:], preferred_element_type=F32)
    loads[2].wait()
    loads[3].wait()

    @pl.when(turn == 0)
    def _():
        history[...] = jnp.zeros_like(history)

    @pl.when(turn > 0)
    def _():
        hist_copy().wait_recv()

    filtered[:, :step] = (
        here + jnp.dot(history[...], band[:LANES], preferred_element_type=F32)
    ).astype(BF16)
    weighted[...] = jnp.dot(filtered[...], sketch[...], preferred_element_type=F32)

    @pl.when(turn > 0)
    def _():
        prev_copy().wait_recv()
        weighted[...] = rates[...] * before[...] + weighted[...]

    @pl.when(turn < batches - 1)
    def _():
        prev_copy().start()

    value = weighted[...]
    gram = jnp.dot(value.T, value, precision=HIGHEST, preferred_element_type=F32)
    half = rank // 2
    blocks = jnp.concatenate([gram[:half, :half], gram[:half, half:], gram[half:, half:]], axis=0)
    for index in range(count):
        parts[index] = cut(blocks, index, parts.shape[1], F32)
    gram_first = exchange(count, lambda peer: parts.at[peer], lambda mine: landed.at[mine], gram_a, gram_b)

    turned = filtered[...].T
    cross = jnp.zeros((frame_count, rank), F32)
    for piece in reversed(pieces(value)):
        cross = cross + jnp.dot(turned, piece.astype(BF16), preferred_element_type=F32)
    outer, inner = groups(count)
    plane, spot = place_of(count)
    shard = cross_total.shape[1]
    for index in range(count):
        cross_parts[index % inner, index // inner] = cut(cross, index, shard, F32)

    landed[row] = parts[row]
    total[row] = sum_slots(landed, gram_first)
    gram_across, gram_within = gather(count, total, gram_c, gram_d)
    ids = lax.broadcasted_iota(jnp.int32, (rank, rank), 0)
    cols = lax.broadcasted_iota(jnp.int32, (rank, rank), 1)
    work[:, rank:] = jnp.where(ids == cols, 1.0, 0.0).astype(F32)
    upper[...] = jnp.zeros_like(upper)
    inverse[...] = jnp.zeros_like(inverse)
    cross_landed[spot] = cross_parts[spot]
    for copy in gram_within:
        copy.wait_recv()
    cross_first = []
    for i in range(1, inner):
        other = lax.rem(spot + i, inner)
        cross_first.append(
            send(cross_parts.at[other], cross_landed.at[spot], cross_a, cross_b, i, plane * inner + other)
        )
    packed = jnp.concatenate([total[index] for index in range(count)], axis=0)
    across = packed[half:rank]
    work[:half, :half] = packed[:half]
    work[:half, half:rank] = across
    work[half:, :half] = across.T
    work[half:, half:rank] = packed[rank : rank + half]
    cross_second = []
    for begin in range(0, rank, LANES):
        eliminate(work, upper, inverse, begin)
        if begin == 0:
            cross_mid[...] = sum_slots(cross_landed, cross_first)
            cross_last[plane] = cross_mid[plane]
            for o in range(1, outer):
                other = lax.rem(plane + o, outer)
                cross_second.append(
                    send(cross_mid.at[other], cross_last.at[plane], cross_c, cross_d, o, other * inner + spot)
                )

    root = math.sqrt(npoints)
    against = (((1,), (1,)), ((), ()))
    mine = sum_slots(cross_last, cross_second) * (math.sqrt(rank) / root)
    cross_total[row] = lax.dot_general(
        mine, inverse[...], against, precision=HIGHEST, preferred_element_type=F32
    ).astype(BF16)
    cross_across, cross_within = gather(count, cross_total, cross_e, cross_f)
    factor[0] = jnp.where(cols >= ids, upper[...], 0.0) * (1.0 / root)
    store_factor = pltpu.make_async_copy(factor, factor_hbm, store_sems.at[0])
    store_factor.start()
    basis[0] = lax.dot_general(
        weighted[...], inverse[...], against, precision=HIGHEST, preferred_element_type=F32
    ) * root
    store_basis = pltpu.make_async_copy(basis, basis_hbm, store_sems.at[1])
    store_basis.start()
    for copy in cross_within:
        copy.wait_recv()
    for index in range(count):
        low = index * shard
        if low < frame_count:
            coeffs[low : low + shard] = cross_total[index]

    store_factor.wait()
    store_basis.wait()
    sent = gram_first + gram_across + gram_within + cross_first + cross_second + cross_across + cross_within
    for copy in sent:
        copy.wait_send()

    @pl.when(turn < batches - 1)
    def _():
        hist_copy().wait_send()
        prev_copy().wait_send()


def pieces(x):
    high = x.astype(BF16).astype(F32)
    rest = x - high
    mid = rest.astype(BF16).astype(F32)
    return high, mid, rest - mid


def eliminate(work, upper, inverse, begin):
    rank = work.shape[0]
    first = begin
    last = rank + begin + LANES
    width = rank - first
    tiles = PANEL // TILE
    full = (TILE, LANES)

    def wide(x, copies):
        return jnp.concatenate([x] * copies, axis=1)

    def panel(index, _):
        offset = pl.multiple_of(index * PANEL, PANEL)
        rows = pl.ds(pl.multiple_of(begin + offset, PANEL), PANEL)
        block = work[rows, first:last]
        corner = pltpu.roll(block[:, :LANES], lax.rem(LANES - offset, LANES), 1)
        block = jnp.concatenate([block, corner], axis=1)
        copies = block.shape[1] // LANES
        body = [block[b * TILE : (b + 1) * TILE] for b in range(tiles)]
        place = lax.broadcasted_iota(jnp.int32, body[0].shape, 0)
        for c in range(tiles):
            columns = [
                [
                    jnp.broadcast_to(body[b][:, at : at + 1], full)
                    for at in range(last - first + c * TILE, last - first + (c + 1) * TILE)
                ]
                for b in range(c, tiles)
            ]
            held = {
                (i, j): jnp.broadcast_to(columns[0][j][i : i + 1], full)
                for j in range(TILE)
                for i in range(j, TILE)
            }
            lines = [jnp.broadcast_to(body[c][i : i + 1], body[c].shape) for i in range(TILE)]
            result = jnp.zeros_like(body[c])
            for j in range(TILE):
                scale = lax.rsqrt(held[j, j])
                factors = {i: held[i, j] * scale for i in range(j + 1, TILE)}
                for i in range(j + 1, TILE):
                    for k in range(j + 1, i + 1):
                        held[i, k] = held[i, k] - factors[i] * factors[k]
                done = lines[j] * wide(scale, copies)
                for i in range(j + 1, TILE):
                    lines[i] = lines[i] - wide(factors[i], copies) * done
                for b in range(c + 1, tiles):
                    down = columns[b - c][j] * scale
                    for k in range(j + 1, TILE):
                        columns[b - c][k] = columns[b - c][k] - down * factors[k]
                    body[b] = body[b] - wide(down, copies) * done
                result = jnp.where(place == j, done, result)
            body[c] = result
        solved = jnp.concatenate(body, axis=0)[:, : last - first]
        upper[rows, first:rank] = solved[:, :width]
        inverse[rows, : begin + LANES] = solved[:, width:]
        high, mid, low = pieces(solved)
        left = jnp.concatenate([high, high, mid, high, mid, low], axis=0)[:, :width].astype(BF16)
        right = jnp.concatenate([high, mid, high, low, mid, high], axis=0).astype(BF16)
        work[first:, first:last] = work[first:, first:last] - lax.dot_general(
            left, right, (((0,), (0,)), ((), ())), preferred_element_type=F32
        )
        return 0

    lax.fori_loop(0, LANES // PANEL, panel, 0)


def finish_kernel(basis, factor, turned, basis_out, factor_out, coeffs_out, done):
    copies = [
        pltpu.make_async_copy(basis, basis_out, done.at[0]),
        pltpu.make_async_copy(factor, factor_out, done.at[1]),
    ]
    for copy in copies:
        copy.start()
    coeffs_out[0] = turned[...].astype(F32).T
    for copy in copies:
        copy.wait()


def shard_rows(length, count, tile):
    return tile * -(-length // (tile * count))


def shards(frames, tap_table, sketch_matrix, decay_rates):
    count, batches = lax.axis_size("rows"), lax.axis_size("batch")
    rows_here, frame_count = frames.shape
    rank = sketch_matrix.shape[1]
    half = rank // 2
    taps = tap_table.reshape(1, -1)
    gram_slots = pltpu.VMEM((count, shard_rows(3 * half, count, 8), half), F32)
    outer, inner = groups(count)
    shard = shard_rows(frame_count, count, 16)
    cross_slots = pltpu.VMEM((inner, outer, shard, rank), F32)
    cross_line = pltpu.VMEM((outer, shard, rank), F32)
    basis, factor, coeffs = pl.pallas_call(
        functools.partial(whole_kernel, count, batches, rows_here * count),
        out_shape=(
            jax.ShapeDtypeStruct((1, rows_here, rank), F32),
            jax.ShapeDtypeStruct((1, rank, rank), F32),
            jax.ShapeDtypeStruct((frame_count, rank), BF16),
        ),
        in_specs=[HBM_SPEC] * 4,
        out_specs=(HBM_SPEC, HBM_SPEC, VMEM_SPEC),
        scratch_shapes=[
            pltpu.VMEM(frames.shape, BF16),
            pltpu.VMEM(taps.shape, jnp.int32),
            pltpu.VMEM(sketch_matrix.shape, BF16),
            pltpu.VMEM(decay_rates.shape, F32),
            pltpu.VMEM((1, 4 * LANES), F32),
            pltpu.VMEM((rows_here, LANES), BF16),
            pltpu.VMEM((rows_here, rank), F32),
            pltpu.VMEM((rows_here, rank), F32),
            pltpu.VMEM((rows_here, frame_count), BF16),
            gram_slots,
            gram_slots,
            gram_slots,
            cross_slots,
            cross_slots,
            cross_line,
            cross_line,
            pltpu.VMEM((count, shard, rank), BF16),
            pltpu.VMEM((rank, 2 * rank), F32),
            pltpu.VMEM((rank, rank), F32),
            pltpu.VMEM((rank, rank), F32),
            pltpu.VMEM((1, rows_here, rank), F32),
            pltpu.VMEM((1, rank, rank), F32),
            pltpu.SemaphoreType.DMA((4,)),
            pltpu.SemaphoreType.DMA((2,)),
            pltpu.SemaphoreType.DMA((2,)),
            pltpu.SemaphoreType.DMA((2,)),
        ] + [pltpu.SemaphoreType.DMA((count,)) for _ in range(10)],
        compiler_params=pltpu.CompilerParams(
            collective_id=0, has_side_effects=True, vmem_limit_bytes=GRANT
        ),
        name="whole",
    )(frames, taps, sketch_matrix, decay_rates)
    return pl.pallas_call(
        finish_kernel,
        out_shape=(
            jax.ShapeDtypeStruct(basis.shape, F32),
            jax.ShapeDtypeStruct(factor.shape, F32),
            jax.ShapeDtypeStruct((1, rank, frame_count), F32),
        ),
        in_specs=[HBM_SPEC, HBM_SPEC, VMEM_SPEC],
        out_specs=(HBM_SPEC, HBM_SPEC, VMEM_SPEC),
        scratch_shapes=[pltpu.SemaphoreType.DMA((2,))],
        compiler_params=pltpu.CompilerParams(vmem_limit_bytes=GRANT),
        name="finish",
    )(basis, factor, coeffs)


def solution(mesh):
    placed = (P("rows", "batch"), P(), P(), P("batch", None))
    return jax.shard_map(
        shards,
        mesh=mesh,
        in_specs=placed,
        out_specs=(P("batch", "rows", None), P("batch", None, None), P("batch", None, None)),
        check_vma=False,
    )
```

profile of v0, /device:TPU:0, one launch (start us, length us, event | category | flops | bytes accessed | tf_op | source)
XLA Modules:
  0.0 64.3 jit_solution(14931100702534507191)
XLA Ops:
  0.6 44.9 %whole.1 = (f32[1,256,256]{2,1,0:T(8,128)}, f32[1,256,256]{2,1,0:T(8,128)}, bf16[512,256]{1,0:T(8,128)(2,1)}) custom-call(bf16[256,512]{1,0:T(8,128)(2,1)} %frames_hbm.1, s32[1,63]{1,0:T(1,128)} %bitcast.1, bf16[512,256]{1,0:T(8,128)(2,1)} %sketch_hbm.1, f32[1,256]{1,0:T(1,128)} %rates_hbm.1), custom_call_target="tpu_custom_call" | custom-call | tf_op jit(solution)/shard_map/whole/pallas_call | solution.py:392
  45.6 18.7 %finish.1 = (f32[1,256,256]{2,1,0:T(8,128)}, f32[1,256,256]{2,1,0:T(8,128)}, f32[1,256,512]{2,1,0:T(8,128)}) custom-call(f32[1,256,256]{2,1,0:T(8,128)} %get-tuple-element.6.basis, f32[1,256,256]{2,1,0:T(8,128)} %get-tuple-element.7.factor, bf16[512,256]{1,0:T(8,128)(2,1)} %get-tuple-element.8.turned), custom_call_target="tpu_custom_call" | custom-call | tf_op jit(solution)/shard_map/finish/pallas_call | solution.py:434
where the time goes:
time: 64.5 us; the launch traced here: 64.3 us
  Pallas kernels  63.7 us (99%)
    pallas_call x1, Pallas kernels, shards(): pl.pallas_call(functools.partial(whole_kernel, count, batches, rows_here...  44.9 us
    pallas_call x1, Pallas kernels, shards(): pl.pallas_call(finish_kernel, out_shape=(jax.ShapeDtypeStruct(basis.shape...  18.7 us

commit v1 on v0

--- a/solution.py
+++ b/solution.py
@@ -220,6 +220,13 @@
     shard = cross_total.shape[1]
     for index in range(count):
         cross_parts[index % inner, index // inner] = cut(cross, index, shard, F32)
+    cross_first = []
+    for i in range(1, inner):
+        other = lax.rem(spot + i, inner)
+        cross_first.append(
+            send(cross_parts.at[other], cross_landed.at[spot], cross_a, cross_b, i, plane * inner + other)
+        )
+    cross_landed[spot] = cross_parts[spot]
 
     landed[row] = parts[row]
     total[row] = sum_slots(landed, gram_first)
@@ -229,14 +236,15 @@
     work[:, rank:] = jnp.where(ids == cols, 1.0, 0.0).astype(F32)
     upper[...] = jnp.zeros_like(upper)
     inverse[...] = jnp.zeros_like(inverse)
-    cross_landed[spot] = cross_parts[spot]
     for copy in gram_within:
         copy.wait_recv()
-    cross_first = []
-    for i in range(1, inner):
-        other = lax.rem(spot + i, inner)
-        cross_first.append(
-            send(cross_parts.at[other], cross_landed.at[spot], cross_a, cross_b, i, plane * inner + other)
+    cross_mid[...] = sum_slots(cross_landed, cross_first)
+    cross_last[plane] = cross_mid[plane]
+    cross_second = []
+    for o in range(1, outer):
+        other = lax.rem(plane + o, outer)
+        cross_second.append(
+            send(cross_mid.at[other], cross_last.at[plane], cross_c, cross_d, o, other * inner + spot)
         )
     packed = jnp.concatenate([total[index] for index in range(count)], axis=0)
     across = packed[half:rank]
@@ -244,17 +252,8 @@
     work[:half, half:rank] = across
     work[half:, :half] = across.T
     work[half:, half:rank] = packed[rank : rank + half]
-    cross_second = []
     for begin in range(0, rank, LANES):
         eliminate(work, upper, inverse, begin)
-        if begin == 0:
-            cross_mid[...] = sum_slots(cross_landed, cross_first)
-            cross_last[plane] = cross_mid[plane]
-            for o in range(1, outer):
-                other = lax.rem(plane + o, outer)
-                cross_second.append(
-                    send(cross_mid.at[other], cross_last.at[plane], cross_c, cross_d, o, other * inner + spot)
-                )
 
     root = math.sqrt(npoints)
     against = (((1,), (1,)), ((), ()))
@@ -362,16 +361,27 @@
     lax.fori_loop(0, LANES // PANEL, panel, 0)
 
 
-def finish_kernel(basis, factor, turned, basis_out, factor_out, coeffs_out, done):
-    copies = [
-        pltpu.make_async_copy(basis, basis_out, done.at[0]),
-        pltpu.make_async_copy(factor, factor_out, done.at[1]),
+def finish_kernel(
+    basis_in, factor_in, turned_in, basis_out, factor_out, coeffs_out, basis, factor, turned, coeffs, loaded, stored
+):
+    loads = [
+        pltpu.make_async_copy(source, target, loaded.at[index])
+        for index, (source, target) in enumerate(((turned_in, turned), (basis_in, basis), (factor_in, factor)))
     ]
-    for copy in copies:
-        copy.start()
-    coeffs_out[0] = turned[...].astype(F32).T
-    for copy in copies:
-        copy.wait()
+    stores = [
+        pltpu.make_async_copy(source, target, stored.at[index])
+        for index, (source, target) in enumerate(((coeffs, coeffs_out), (basis, basis_out), (factor, factor_out)))
+    ]
+    for load in loads:
+        load.start()
+    for index in (1, 2):
+        loads[index].wait()
+        stores[index].start()
+    loads[0].wait()
+    coeffs[0] = turned[...].astype(F32).T
+    stores[0].start()
+    for store in stores:
+        store.wait()
 
 
 def shard_rows(length, count, tile):
@@ -438,9 +448,16 @@
             jax.ShapeDtypeStruct(factor.shape, F32),
             jax.ShapeDtypeStruct((1, rank, frame_count), F32),
         ),
-        in_specs=[HBM_SPEC, HBM_SPEC, VMEM_SPEC],
-        out_specs=(HBM_SPEC, HBM_SPEC, VMEM_SPEC),
-        scratch_shapes=[pltpu.SemaphoreType.DMA((2,))],
+        in_specs=[HBM_SPEC] * 3,
+        out_specs=(HBM_SPEC,) * 3,
+        scratch_shapes=[
+            pltpu.VMEM(basis.shape, F32),
+            pltpu.VMEM(factor.shape, F32),
+            pltpu.VMEM(coeffs.shape, BF16),
+            pltpu.VMEM((1, rank, frame_count), F32),
+            pltpu.SemaphoreType.DMA((3,)),
+            pltpu.SemaphoreType.DMA((3,)),
+        ],
         compiler_params=pltpu.CompilerParams(vmem_limit_bytes=GRANT),
         name="finish",
     )(basis, factor, coeffs)

time: 64.5 us -> 44.1 us (0.68)
  Pallas kernels: 63.7 us -> 43.3 us
    pallas_call x1, Pallas kernels: 18.7 us -> 2.1 us  [shards(): pl.pallas_call(finish_kernel, out_shape=(jax.ShapeDtypeStruct(basis.shape...]
    pallas_call x1, Pallas kernels: 44.9 us -> 41.2 us  [shards(): pl.pallas_call(functools.partial(whole_kernel, count, batches, rows_here...]
where the time goes in v1:
time: 44.1 us; the launch traced here: 44 us
  Pallas kernels  43.3 us (98%)
  between operations  0.64 us (1%)
    pallas_call x1, Pallas kernels, shards(): pl.pallas_call(functools.partial(whole_kernel, count, batches, rows_here...  41.2 us
    pallas_call x1, Pallas kernels, shards(): pl.pallas_call(finish_kernel, out_shape=(jax.ShapeDtypeStruct(basis.shape...  2.1 us

profile of v1, /device:TPU:0, one launch (start us, length us, event | category | flops | bytes accessed | tf_op | source)
XLA Modules:
  0.0 44.0 jit_solution(12381236540488749125)
XLA Ops:
  0.6 41.2 %whole.1 = (f32[1,256,256]{2,1,0:T(8,128)}, f32[1,256,256]{2,1,0:T(8,128)}, bf16[512,256]{1,0:T(8,128)(2,1)}) custom-call(bf16[256,512]{1,0:T(8,128)(2,1)} %frames_hbm.1, s32[1,63]{1,0:T(1,128)} %bitcast.1, bf16[512,256]{1,0:T(8,128)(2,1)} %sketch_hbm.1, f32[1,256]{1,0:T(1,128)} %rates_hbm.1), custom_call_target="tpu_custom_call" | custom-call | tf_op jit(solution)/shard_map/whole/pallas_call | solution.py:402
  41.9 2.1 %finish.1 = (f32[1,256,256]{2,1,0:T(8,128)}, f32[1,256,256]{2,1,0:T(8,128)}, f32[1,256,512]{2,1,0:T(8,128)}) custom-call(f32[1,256,256]{2,1,0:T(8,128)} %get-tuple-element.6.basis_in, f32[1,256,256]{2,1,0:T(8,128)} %get-tuple-element.7.factor_in, bf16[512,256]{1,0:T(8,128)(2,1)} %get-tuple-element.8.turned_in), custom_call_target="tpu_custom_call" | custom-call | tf_op jit(solution)/shard_map/finish/pallas_call | solution.py:444

commit v2 on v1

--- a/solution.py
+++ b/solution.py
@@ -122,8 +122,8 @@
     count, batches, npoints,
     frames_hbm, taps_hbm, sketch_hbm, rates_hbm, basis_hbm, factor_hbm, coeffs,
     frames, taps, sketch, rates, tap_row, history, before, weighted, filtered,
-    parts, landed, total, cross_parts, cross_landed, cross_mid, cross_last, cross_total, work, upper, inverse, basis, factor,
-    load_sems, store_sems, hist_sems, prev_sems, gram_a, gram_b, gram_c, gram_d, cross_a, cross_b, cross_c, cross_d, cross_e, cross_f,
+    parts, landed, total, late_parts, late_landed, late_total, cross_parts, cross_landed, cross_mid, cross_last, cross_total, work, upper, inverse, basis, factor,
+    load_sems, store_sems, hist_sems, prev_sems, gram_a, gram_b, gram_c, gram_d, late_a, late_b, late_c, late_d, cross_a, cross_b, cross_c, cross_d, cross_e, cross_f,
 ):
     row, turn = lax.axis_index("rows"), lax.axis_index("batch")
     frame_count = frames.shape[1]
@@ -206,10 +206,16 @@
     value = weighted[...]
     gram = jnp.dot(value.T, value, precision=HIGHEST, preferred_element_type=F32)
     half = rank // 2
-    blocks = jnp.concatenate([gram[:half, :half], gram[:half, half:], gram[half:, half:]], axis=0)
+    blocks = jnp.concatenate([gram[:half, :half], gram[:half, half:]], axis=0)
+    corner = gram[half:, half:]
     for index in range(count):
         parts[index] = cut(blocks, index, parts.shape[1], F32)
     gram_first = exchange(count, lambda peer: parts.at[peer], lambda mine: landed.at[mine], gram_a, gram_b)
+    for index in range(count):
+        late_parts[index] = cut(corner, index, late_parts.shape[1], F32)
+    late_first = exchange(
+        count, lambda peer: late_parts.at[peer], lambda mine: late_landed.at[mine], late_a, late_b
+    )
 
     turned = filtered[...].T
     cross = jnp.zeros((frame_count, rank), F32)
@@ -231,6 +237,11 @@
     landed[row] = parts[row]
     total[row] = sum_slots(landed, gram_first)
     gram_across, gram_within = gather(count, total, gram_c, gram_d)
+    late_landed[row] = late_parts[row]
+    late_total[row] = sum_slots(late_landed, late_first)
+    late_second = exchange(
+        count, lambda peer: late_total.at[row], lambda mine: late_total.at[mine], late_c, late_d
+    )
     ids = lax.broadcasted_iota(jnp.int32, (rank, rank), 0)
     cols = lax.broadcasted_iota(jnp.int32, (rank, rank), 1)
     work[:, rank:] = jnp.where(ids == cols, 1.0, 0.0).astype(F32)
@@ -251,9 +262,13 @@
     work[:half, :half] = packed[:half]
     work[:half, half:rank] = across
     work[half:, :half] = across.T
-    work[half:, half:rank] = packed[rank : rank + half]
-    for begin in range(0, rank, LANES):
-        eliminate(work, upper, inverse, begin)
+    work[half:, half:rank] = jnp.zeros((half, half), F32)
+    eliminate(work, upper, inverse, 0)
+    for copy in late_second:
+        copy.wait_recv()
+    corner = jnp.concatenate([late_total[index] for index in range(count)], axis=0)
+    work[half:, half:rank] = work[half:, half:rank] + corner[:half]
+    eliminate(work, upper, inverse, half)
 
     root = math.sqrt(npoints)
     against = (((1,), (1,)), ((), ()))
@@ -279,7 +294,7 @@
 
     store_factor.wait()
     store_basis.wait()
-    sent = gram_first + gram_across + gram_within + cross_first + cross_second + cross_across + cross_within
+    sent = late_first + late_second + gram_first + gram_across + gram_within + cross_first + cross_second + cross_across + cross_within
     for copy in sent:
         copy.wait_send()
 
@@ -394,7 +409,8 @@
     rank = sketch_matrix.shape[1]
     half = rank // 2
     taps = tap_table.reshape(1, -1)
-    gram_slots = pltpu.VMEM((count, shard_rows(3 * half, count, 8), half), F32)
+    gram_slots = pltpu.VMEM((count, shard_rows(2 * half, count, 8), half), F32)
+    late_slots = pltpu.VMEM((count, shard_rows(half, count, 8), half), F32)
     outer, inner = groups(count)
     shard = shard_rows(frame_count, count, 16)
     cross_slots = pltpu.VMEM((inner, outer, shard, rank), F32)
@@ -421,6 +437,9 @@
             gram_slots,
             gram_slots,
             gram_slots,
+            late_slots,
+            late_slots,
+            late_slots,
             cross_slots,
             cross_slots,
             cross_line,
@@ -435,7 +454,7 @@
             pltpu.SemaphoreType.DMA((2,)),
             pltpu.SemaphoreType.DMA((2,)),
             pltpu.SemaphoreType.DMA((2,)),
-        ] + [pltpu.SemaphoreType.DMA((count,)) for _ in range(10)],
+        ] + [pltpu.SemaphoreType.DMA((count,)) for _ in range(14)],
         compiler_params=pltpu.CompilerParams(
             collective_id=0, has_side_effects=True, vmem_limit_bytes=GRANT
         ),

time: 44.1 us -> 44.1 us (level)
  no operation moved by 1% of the time
where the time goes in v2:
time: 44.1 us; the launch traced here: 44 us
  Pallas kernels  43.3 us (98%)
  between operations  0.64 us (1%)
    pallas_call x1, Pallas kernels, shards(): pl.pallas_call(functools.partial(whole_kernel, count, batches, rows_here...  41.2 us
    pallas_call x1, Pallas kernels, shards(): pl.pallas_call(finish_kernel, out_shape=(jax.ShapeDtypeStruct(basis.shape...  2.1 us

profile of v2, /device:TPU:0, one launch (start us, length us, event | category | flops | bytes accessed | tf_op | source)
XLA Modules:
  0.0 44.0 jit_solution(14171010388524939597)
XLA Ops:
  0.6 41.2 %whole.1 = (f32[1,256,256]{2,1,0:T(8,128)}, f32[1,256,256]{2,1,0:T(8,128)}, bf16[512,256]{1,0:T(8,128)(2,1)}) custom-call(bf16[256,512]{1,0:T(8,128)(2,1)} %frames_hbm.1, s32[1,63]{1,0:T(1,128)} %bitcast.1, bf16[512,256]{1,0:T(8,128)(2,1)} %sketch_hbm.1, f32[1,256]{1,0:T(1,128)} %rates_hbm.1), custom_call_target="tpu_custom_call" | custom-call | tf_op jit(solution)/shard_map/whole/pallas_call | solution.py:418
  41.9 2.1 %finish.1 = (f32[1,256,256]{2,1,0:T(8,128)}, f32[1,256,256]{2,1,0:T(8,128)}, f32[1,256,512]{2,1,0:T(8,128)}) custom-call(f32[1,256,256]{2,1,0:T(8,128)} %get-tuple-element.6.basis_in, f32[1,256,256]{2,1,0:T(8,128)} %get-tuple-element.7.factor_in, bf16[512,256]{1,0:T(8,128)(2,1)} %get-tuple-element.8.turned_in), custom_call_target="tpu_custom_call" | custom-call | tf_op jit(solution)/shard_map/finish/pallas_call | solution.py:463
